TPU v7x, 256 devices: a whole 4x4x8 slice. The times are simulated.
256 devices in a mesh: row: 16 (over x, y), col: 16 (over z, core).
Axes of the slice: x: 4, y: 4, z: 8, core: 2. Of those that a mesh axis runs over, the one named last changes fastest.
Arguments:
- src_points: float32 [73728, 64], P('row'), may hold values from -1.2 to 1.2
- dst_points: float32 [73728, 64], P(('col', 'row')), may hold values from -1.2 to 1.2
- dst_potential: float32 [73728], P(('col', 'row')), may hold values from -1.2 to 25.3
- partners: int32 [288, 28], P('row'), may hold values from 0 to 287, as said below
- partner_count: int32 [288], P('row'), may hold values from 14 to 28
- src_count: int32 [288], P('row'), may hold values from 64 to 256
- dst_count: int32 [288], P('col'), may hold values from 64 to 256
Outputs:
- src_potential: float32 [73728], P('row')
- dst_new: float32 [73728], P(('col', 'row'))
Inputs may be any that keep to these rules, and one draw needn't show every extreme that they name: `partners`: row s holds 28 different tiles, each within 28 tiles of tile s * 1, counted around the end of the range, except that for even s slot 0 holds tile (s * 1 + 288 // 2) mod 288.
All inputs are finite; a program needn't handle non-finite values.
Results may differ from a plain program's by a relative error of at most 0.00029.
Values sent between devices are 32-bit elements; how exact they have to be, the bound alone decides.
No kernel may reach another device: no remote copies, remote signals or barrier semaphores. Data moves between devices by JAX's collectives and lax.ppermute only.
A program may use at most 128 MiB of HBM per device.

v0:
```python
import functools
import math

import jax
import jax.numpy as jnp
from jax import lax
from jax.experimental import pallas as pl
from jax.experimental.pallas import tpu as pltpu
from jax.sharding import PartitionSpec as P

entropy = 0.1
scale = math.log2(math.e) / entropy
ln2 = math.log(2.0)
nothing = -1e30
floor = -1e25
unit_rows = 64
group = 12
ring = 4
f32 = jnp.float32
bf16 = jnp.bfloat16


def pieces(a):
    first = a.astype(bf16).astype(f32)
    rest = a - first
    second = rest.astype(bf16).astype(f32)
    return first, second, rest - second


def extra_rows(bias):
    place = lax.broadcasted_iota(jnp.int32, (64, bias.shape[1]), 0)
    block = jnp.where(place < 3, 1.0, 0.0)
    for k, piece in enumerate(pieces(bias)):
        block = jnp.where(place == 3 + k, piece, block)
    return block.astype(bf16)


def pack_targets(count_ref, points_ref, potential_ref, wire_ref, square_ref, line_ref):
    share = points_ref.shape[1]
    tile = 256
    mid = share // 2
    begin = lax.axis_index("row") * share
    first_tile = begin // tile
    offset = begin - first_tile * tile
    last_tile = jnp.minimum(first_tile + 1, count_ref.shape[0] - 1)
    points = points_ref[...]
    square_ref[...] = jnp.zeros_like(square_ref)
    square_ref[0:64, 0:share] = points
    turned = square_ref[...].T
    wire_ref[0:mid, :] = scale * (turned[0:mid] + pltpu.roll(turned[mid:share], 64, 1))
    level = scale * (potential_ref[...] - 0.5 * jnp.sum(points * points, axis=0, keepdims=True))
    spot = offset + lax.broadcasted_iota(jnp.int32, (1, share), 1)
    place = jnp.where(spot < tile, spot, spot - tile)
    bound = jnp.where(spot < tile, count_ref[first_tile], count_ref[last_tile])
    line_ref[...] = jnp.full_like(line_ref, nothing)
    line_ref[0:1, 0:share] = jnp.where(place < bound, level, nothing)
    wire_ref[mid : mid + 8, :] = jnp.zeros((8, 128), f32)
    for k in range(3):
        wire_ref[mid + k : mid + k + 1, :] = line_ref[0:1, 128 * k : 128 * (k + 1)]


def unpack_targets(held_ref, arrived, operand_ref):
    lane = lax.broadcasted_iota(jnp.int32, (144, 128), 1)
    front = lane < 64
    sublane = lax.broadcasted_iota(jnp.int32, (16, 384), 0)
    pick_row = lax.broadcasted_iota(jnp.int32, (16, 128), 0)
    pick_lane = lax.broadcasted_iota(jnp.int32, (16, 128), 1)
    pick = jnp.where((pick_lane == pick_row + 64) & (pick_row < 6), 1.0, 0.0).astype(bf16)
    row_here = lax.axis_index("row")
    x_here = row_here // ring
    y_here = row_here - x_here * ring
    even = lax.rem(lax.axis_index("col"), 2) == 0
    for k in range(ring):
        arrived(k)
        for j in range(ring):
            x = lax.rem(x_here + ring - jnp.where(even, k, j), ring)
            y = lax.rem(y_here + ring - jnp.where(even, j, k), ring)
            a = pl.multiple_of((x * ring + y) * 288, 16)
            b = pl.multiple_of((x * ring + y) * 288 + 144, 16)
            both = held_ref[k, j, 0:144, :]
            high = both.astype(bf16).astype(f32)
            low = both - high
            high_back = pltpu.roll(high, 64, 1)
            low_back = pltpu.roll(low, 64, 1)
            tail = held_ref[k, j, 144:152, :]
            line = jnp.concatenate([tail[0:1], tail[1:2], tail[2:3]], axis=1)
            stacked = jnp.where(sublane < 6, 1.0, 0.0)
            for i, piece in enumerate(pieces(line)):
                stacked = jnp.where(sublane == i, piece, stacked)
            extra = lax.dot_general(
                stacked.astype(bf16), pick, (((0,), (0,)), ((), ())), preferred_element_type=f32
            )
            operand_ref[pl.ds(a, 144), 0:128] = jnp.where(front, high, low_back).astype(bf16)
            operand_ref[pl.ds(a, 144), 128:256] = jnp.where(front, high, extra[0:144]).astype(bf16)
            operand_ref[pl.ds(b, 144), 0:128] = jnp.where(front, high_back, low).astype(bf16)
            operand_ref[pl.ds(b, 144), 128:256] = jnp.where(
                front, high_back, extra[144:288]
            ).astype(bf16)
    rows = ring * ring * 288
    dummy_lane = lax.broadcasted_iota(jnp.int32, (unit_rows, 256), 1)
    operand_ref[rows : rows + unit_rows, :] = jnp.where(dummy_lane == 192, nothing, 0.0).astype(bf16)


def load_weights(points_ref, weights_ref, shift):
    tiles, depth, tile = weights_ref.shape
    for s in range(tiles):
        x = points_ref[:, s * tile : (s + 1) * tile]
        high = x.astype(bf16)
        low = (x - high.astype(f32)).astype(bf16)
        bias = (-0.5 * scale) * jnp.sum(x * x, axis=0, keepdims=True)
        weights_ref[s, 0:64, :] = high
        weights_ref[s, 64:128, :] = high
        weights_ref[s, 128:192, :] = low
        weights_ref[s, 192:256, :] = extra_rows(bias if shift is None else bias + shift[s : s + 1, :])


def load_all(points_ref, shift, wires, held_ref, sems, operand_ref, weights_ref):
    copies = [
        pltpu.make_async_copy(wire, held_ref.at[k], sems.at[k]) for k, wire in enumerate(wires)
    ]
    for copy in copies:
        copy.start()
    load_weights(points_ref, weights_ref, shift)
    unpack_targets(held_ref, lambda k: copies[k].wait(), operand_ref)


def pipeline(item_ref, list_ref, items, operand_ref, weights_ref, buffers, visit):
    per = list_ref.shape[1] // group
    last = weights_ref.shape[0] - 1

    def where(i):
        code = item_ref[i]
        s = code // per
        first = (code - s * per) * group
        return jnp.minimum(s, last), [list_ref[s, first + k] for k in range(group)]

    def multiply(i, buffer):
        s, units = where(i)
        rows = jnp.concatenate(
            [
                operand_ref[pl.ds(pl.multiple_of(u * unit_rows, unit_rows), unit_rows), :]
                for u in units
            ],
            axis=0,
        )
        buffer[...] = jnp.dot(rows, weights_ref[s], preferred_element_type=f32)

    one, two = buffers
    multiply(0, one)

    def step(j, carry):
        multiply(2 * j + 1, two)
        visit(*where(2 * j), one)
        multiply(2 * j + 2, one)
        visit(*where(2 * j + 1), two)
        return carry

    lax.fori_loop(0, (items + 1) // 2, step, 0)


def row_pass(
    items_ref, item_ref, count_ref, list_ref, points_ref, need_ref, w0, w1, w2, w3, lse_ref,
    held_ref, sems, operand_ref, weights_ref, one, two, total_ref,
):
    tiles, depth, tile = weights_ref.shape

    @pl.when(items_ref[0] == 0)
    def _():
        lse_ref[...] = jnp.full_like(lse_ref, nothing)

    @pl.when(items_ref[0] > 0)
    def _():
        load_all(points_ref, None, (w0, w1, w2, w3), held_ref, sems, operand_ref, weights_ref)
        total_ref[...] = jnp.zeros_like(total_ref)

        def visit(s, units, buffer):
            part = jnp.exp2(buffer[...]).reshape(4, unit_rows * group // 32, 8, tile)
            total_ref[s] += jnp.sum(jnp.sum(part, axis=1), axis=0)

        pipeline(item_ref, list_ref, items_ref[0], operand_ref, weights_ref, (one, two), visit)
        total = jnp.sum(total_ref[...], axis=1)
        lse_ref[...] = jnp.where(total > 0.0, jnp.log2(jnp.maximum(total, 1e-37)), nothing)
        fine = (total > 1e-25) & (total < 1e30)
        bad = jnp.where(fine, 0.0, need_ref[...])

        @pl.when(jnp.max(bad) > 0.0)
        def _():
            def one_tile(s, carry):
                weights = weights_ref[s]

                def step(i, state):
                    high, total = state
                    unit = list_ref[s, i]
                    rows = operand_ref[
                        pl.ds(pl.multiple_of(unit * unit_rows, unit_rows), unit_rows), :
                    ]
                    score = jnp.dot(rows, weights, preferred_element_type=f32)
                    score = score.reshape(unit_rows // 8, 8, tile)
                    new = jnp.maximum(high, jnp.max(score, axis=0))
                    total = total * jnp.exp2(high - new)
                    return new, total + jnp.sum(jnp.exp2(score - new[None]), axis=0)

                start = (jnp.full((8, tile), floor, f32), jnp.zeros((8, tile), f32))
                high, total = lax.fori_loop(0, count_ref[s], step, start)
                top = jnp.max(high, axis=0, keepdims=True)
                total = jnp.sum(total * jnp.exp2(high - top), axis=0, keepdims=True)
                lse_ref[pl.ds(s, 1), :] = jnp.where(
                    total > 0.0, top + jnp.log2(jnp.maximum(total, 1e-37)), nothing
                )
                return carry

            lax.fori_loop(0, tiles, one_tile, 0)


def column_pass(
    items_ref, item_ref, count_ref, list_ref, points_ref, need_ref, w0, w1, w2, w3, lse_ref,
    mass_ref, other_ref, out_ref, held_ref, sems, operand_ref, weights_ref, one, two, total_ref, high_ref,
):
    tiles, depth, tile = weights_ref.shape

    @pl.when(items_ref[0] == 0)
    def _():
        out_ref[...] = other_ref[...]

    @pl.when(items_ref[0] > 0)
    def _():
        shift = mass_ref[...] - lse_ref[...]
        load_all(points_ref, shift, (w0, w1, w2, w3), held_ref, sems, operand_ref, weights_ref)
        total_ref[...] = jnp.zeros_like(total_ref)

        def visit(s, units, buffer):
            for k, u in enumerate(units):
                where = pl.ds(pl.multiple_of(u * unit_rows, unit_rows), unit_rows)
                part = jnp.exp2(buffer[k * unit_rows : (k + 1) * unit_rows, :])
                total_ref[where, :] += part[:, 0:128] + part[:, 128:256]

        pipeline(item_ref, list_ref, items_ref[0], operand_ref, weights_ref, (one, two), visit)
        eye = lax.broadcasted_iota(jnp.int32, (128, 128), 0) == lax.broadcasted_iota(
            jnp.int32, (128, 128), 1
        )

        def to_row(column):
            return jnp.sum(jnp.where(eye, column, 0.0), axis=0, keepdims=True)

        bad = jnp.zeros((1, 128), f32)
        for u in range(out_ref.shape[0]):
            sums = to_row(jnp.sum(total_ref[u * 128 : (u + 1) * 128, :], axis=1, keepdims=True))
            out_ref[u : u + 1, :] = jnp.where(
                sums > 0.0, jnp.log2(jnp.maximum(sums, 1e-37)), nothing
            )
            bad = jnp.maximum(bad, jnp.where(sums > 1e-25, 0.0, need_ref[u : u + 1, :]))

        @pl.when(jnp.max(bad) > 0.0)
        def _():
            total_ref[...] = jnp.zeros_like(total_ref)
            high_ref[...] = jnp.full_like(high_ref, floor)

            def one_tile(s, carry):
                def step(i, inner):
                    unit = list_ref[s, i]
                    where = pl.ds(pl.multiple_of(unit * unit_rows, unit_rows), unit_rows)
                    score = jnp.dot(
                        operand_ref[where, :], weights_ref[s], preferred_element_type=f32
                    )
                    a, b = score[:, 0:128], score[:, 128:256]
                    old = high_ref[where, :]
                    new = jnp.maximum(old, jnp.maximum(a, b))
                    high_ref[where, :] = new
                    total_ref[where, :] = (
                        total_ref[where, :] * jnp.exp2(old - new)
                        + jnp.exp2(a - new)
                        + jnp.exp2(b - new)
                    )
                    return inner

                lax.fori_loop(0, count_ref[s], step, 0)
                return carry

            lax.fori_loop(0, tiles, one_tile, 0)

            def finish(u, carry):
                where = pl.ds(pl.multiple_of(u * 128, 128), 128)
                high = high_ref[where, :]
                top = jnp.max(high, axis=1, keepdims=True)
                rest = total_ref[where, :] * jnp.exp2(high - top)
                sums = to_row(jnp.sum(rest, axis=1, keepdims=True))
                out_ref[pl.ds(u, 1), :] = jnp.where(
                    sums > 0.0, to_row(top) + jnp.log2(jnp.maximum(sums, 1e-37)), nothing
                )
                return carry

            lax.fori_loop(0, out_ref.shape[0], finish, 0)


def log_sum(parts):
    top = functools.reduce(jnp.maximum, parts)
    total = sum(jnp.exp2(p - top) for p in parts)
    return top + jnp.log2(total)


def work_lists(partners, partner_count, dst_count, col_here):
    src_tiles, slots = partners.shape
    dst_tiles = dst_count.shape[0]
    per_tile = 256 // unit_rows
    units = dst_tiles * per_tile
    per = -(-units // group)
    slot_on = jnp.arange(slots, dtype=jnp.int32)[None, :] < partner_count[:, None]
    local = jnp.where(slot_on, partners - col_here * dst_tiles, -1)
    unit_ids = jnp.arange(units, dtype=jnp.int32)
    unit_tile = unit_ids // per_tile
    live = jnp.repeat(dst_count, per_tile) > (unit_ids % per_tile) * unit_rows
    active = jnp.any(local[:, :, None] == unit_tile[None, None, :], axis=1) & live[None, :]
    earlier = unit_ids[:, None] < unit_ids[None, :]
    rank = jnp.sum((active[:, :, None] & earlier[None]).astype(jnp.int32), axis=1)
    counts = jnp.sum(active.astype(jnp.int32), axis=1)
    order = jnp.arange(per * group, dtype=jnp.int32)
    listed = jnp.sum(
        jnp.where(
            active[:, :, None] & (rank[:, :, None] == order[None, None, :]),
            unit_ids[None, :, None] - units,
            0,
        ),
        axis=1,
    ) + units
    listed = jnp.concatenate([listed, jnp.full((1, per * group), units, jnp.int32)], axis=0)
    chunks = (counts + group - 1) // group
    tile_ids = jnp.arange(src_tiles, dtype=jnp.int32)
    first = jnp.sum(jnp.where(tile_ids[None, :] < tile_ids[:, None], chunks[None, :], 0), axis=1)
    within = jnp.arange(per, dtype=jnp.int32)
    spot = jnp.where(within[None, :] < chunks[:, None], first[:, None] + within[None, :], -1)
    code = tile_ids[:, None] * per + within[None, :] - src_tiles * per
    length = src_tiles * per + 2
    hit = spot.reshape(-1)[:, None] == jnp.arange(length, dtype=jnp.int32)[None, :]
    items = jnp.sum(jnp.where(hit, code.reshape(-1)[:, None], 0), axis=0) + src_tiles * per
    wanted = jnp.any(local[:, :, None] == jnp.arange(dst_tiles, dtype=jnp.int32), axis=1)
    return jnp.sum(chunks), items, counts, listed, wanted


def roles(parity, cols):
    four = [d % cols for d in ((-2, -1, 0, 1), (-1, 0, 1, 2))[parity]]
    lead = [0, (1, -1)[parity] % cols]
    near = lead + [d for d in four if d not in lead]
    out = [(2, -2)[parity] % cols, cols // 2]
    return near, out + [d for d in range(cols) if d not in near and d not in out]


def shards(src_points, dst_points, dst_potential, partners, partner_count, src_count, dst_count):
    src_tiles = src_count.shape[0]
    dst_tiles = dst_count.shape[0]
    tile = src_points.shape[0] // src_tiles
    rows = lax.axis_size("row")
    cols = lax.axis_size("col")
    row_here = lax.axis_index("row")
    col_here = lax.axis_index("col")
    share = dst_points.shape[0]
    points = dst_tiles * tile
    smem = pl.BlockSpec(memory_space=pltpu.SMEM)
    vmem = pl.BlockSpec(memory_space=pltpu.VMEM)
    anywhere = pl.BlockSpec(memory_space=pl.ANY)
    params = pltpu.CompilerParams(vmem_limit_bytes=24 * 1024 * 1024)
    places = [roles(r % 2, cols) for r in range(rows)]
    near = [[(r + d) % cols for d in places[r][0]] for r in range(rows)]
    far = [[(r + d) % cols for d in places[r][1]] for r in range(rows)]
    turn = [
        0 if d in places[p][0] else 1 + places[p][1].index(d) // 4
        for p in range(2)
        for d in range(cols)
    ]
    at = row_here % 2 * cols + (col_here - row_here) % cols
    role = jnp.sum(
        jnp.where(jnp.arange(2 * cols) == at, jnp.array(turn, jnp.int32), 0), dtype=jnp.int32
    )
    in_near = role == 0

    def send(a, hops):
        return lax.ppermute(a, ("row", "col"), [(s[0] * cols + s[1], d[0] * cols + d[1]) for s, d in hops])

    every = [(r, c) for r in range(rows) for c in range(cols)]

    wire = pl.pallas_call(
        pack_targets,
        out_shape=jax.ShapeDtypeStruct((share // 2 + 8, 128), f32),
        in_specs=[smem, vmem, vmem],
        out_specs=vmem,
        scratch_shapes=[pltpu.VMEM((128, 384), f32), pltpu.VMEM((8, 384), f32)],
        compiler_params=params,
    )(dst_count, dst_points.T, dst_potential[None, :])

    def around(r, dx, dy):
        return (r // ring + dx) % ring * ring + (r + dy) % ring

    def first_hop(r, c, k):
        return around(r, 0, k) if c % 2 == 0 else around(r, k, 0)

    def second_hop(r, c, k):
        return around(r, k, 0) if c % 2 == 0 else around(r, 0, k)

    bundle = jnp.stack(
        [wire]
        + [send(wire, [((r, c), (first_hop(r, c, k), c)) for r, c in every]) for k in (1, 2, 3)]
    )
    bundle, partners, partner_count, dst_count, src_count = lax.optimization_barrier(
        (bundle, partners, partner_count, dst_count, src_count)
    )
    busy = [set(near[r] + far[r][:2]) for r in range(rows)]
    wires = [bundle] + [
        send(
            bundle,
            [
                ((r, c), (second_hop(r, c, k), c))
                for r, c in every
                if c in busy[second_hop(r, c, k)]
            ],
        )
        for k in (1, 2, 3)
    ]

    total_items, items, counts, listed, wanted = work_lists(
        partners, partner_count, dst_count, col_here
    )
    near_items = jnp.where(in_near, total_items, 0)[None]
    far_items = jnp.where(in_near, 0, total_items)[None]
    place = jnp.arange(tile, dtype=jnp.int32)
    src_live = place[None, :] < src_count[:, None]
    dst_live = place[None, :] < dst_count[:, None]
    src_need = jnp.where(src_live & (counts > 0)[:, None], 1.0, 0.0)
    dst_need = jnp.where(dst_live & jnp.any(wanted, axis=0)[:, None], 1.0, 0.0)
    dst_need = dst_need.reshape(points // 128, 128)
    counted = src_count.astype(f32)
    all_src = src_tiles * rows
    mass = jnp.where(src_live, -jnp.log2(counted)[:, None] - math.log2(all_src), nothing)

    scratch = [
        pltpu.VMEM((ring, ring) + wire.shape, f32),
        pltpu.SemaphoreType.DMA((ring,)),
        pltpu.VMEM((points + unit_rows, 256), bf16),
        pltpu.VMEM((src_tiles, 256, tile), bf16),
        pltpu.VMEM((unit_rows * group, tile), f32),
        pltpu.VMEM((unit_rows * group, tile), f32),
    ]
    heavy = pl.CostEstimate(flops=8_000_000_000, bytes_accessed=4_000_000, transcendentals=8_000_000)
    light = pl.CostEstimate(flops=100_000_000, bytes_accessed=100_000, transcendentals=100_000)
    turned = src_points.T

    def sum_rows(amount, cost):
        return pl.pallas_call(
            row_pass,
            out_shape=jax.ShapeDtypeStruct((src_tiles, tile), f32),
            in_specs=[smem] * 4 + [vmem] * 2 + [anywhere] * ring,
            out_specs=vmem,
            scratch_shapes=scratch + [pltpu.VMEM((src_tiles, 8, tile), f32)],
            compiler_params=params,
            cost_estimate=cost,
        )(amount, items, counts, listed, turned, src_need, *wires)

    def sum_columns(amount, lse, other, cost):
        return pl.pallas_call(
            column_pass,
            out_shape=jax.ShapeDtypeStruct((points // 128, 128), f32),
            in_specs=[smem] * 4 + [vmem] * 2 + [anywhere] * ring + [vmem] * 3,
            out_specs=vmem,
            scratch_shapes=scratch + [pltpu.VMEM((points + unit_rows, 128), f32)] * 2,
            compiler_params=params,
            cost_estimate=cost,
        )(amount, items, counts, listed, turned, dst_need, *wires, lse, mass, other)

    far_lse = sum_rows(far_items, light)
    early = send(far_lse, [((r, far[r][k]), (r, near[r][k])) for r in range(rows) for k in (0, 1)])
    near_lse = sum_rows(near_items, heavy)
    got_early = (col_here == row_here) | (col_here == row_here + 1 - 2 * (row_here % 2))
    lse = log_sum([near_lse, jnp.where(got_early, early, nothing)])
    lse = log_sum([lse, send(lse, [((r, c), (r, c ^ 1)) for r, c in every])])
    lse = log_sum(
        [
            lse,
            send(
                lse,
                [
                    ((r, c), (r, d))
                    for r in range(rows)
                    for c in near[r]
                    for d in near[r]
                    if (c - d) % cols in (2, cols - 2)
                ],
            ),
        ]
    )
    def final(a, j):
        return send(
            a, [((r, near[r][k]), (r, far[r][4 * j + k])) for r in range(rows) for k in range(4)]
        )

    blank = jnp.full((points // 128, 128), nothing, f32)
    finals = [final(lse, 0)]
    near_part = sum_columns(near_items, lse, blank, heavy)
    late, near_part = lax.optimization_barrier((lse, near_part))
    finals += [final(late, 1), final(late, 2)]
    col_part = sum_columns(far_items, finals[0], near_part, light)
    shared_out = lax.all_to_all(col_part.reshape(rows, share), "row", 0, 0)

    row_lse = lse
    for j in range(3):
        row_lse = jnp.where(role == j + 1, finals[j], row_lse)
    src_potential = jnp.where(
        src_live,
        entropy * (-jnp.log(counted)[:, None] - math.log(all_src) - ln2 * row_lse),
        0.0,
    ).reshape(-1)

    spot = row_here * share + jnp.arange(share, dtype=jnp.int32)
    spot_tile = spot // tile
    spot_count = jnp.sum(
        jnp.where(
            spot_tile[:, None] == jnp.arange(dst_tiles, dtype=jnp.int32)[None, :],
            dst_count[None, :],
            0,
        ),
        axis=1,
    )
    top = jnp.max(shared_out, axis=0)
    col_log = top + jnp.log2(jnp.sum(jnp.exp2(shared_out - top[None]), axis=0))
    dst_new = jnp.where(
        (spot - spot_tile * tile < spot_count) & (top > 0.5 * nothing),
        entropy
        * (-jnp.log(spot_count.astype(f32)) - math.log(dst_tiles * cols) - ln2 * col_log)
        + dst_potential,
        0.0,
    )
    return src_potential, dst_new


def solution(mesh):
    in_specs = (
        P("row", None),
        P(("col", "row"), None),
        P(("col", "row")),
        P("row", None),
        P("row"),
        P("row"),
        P("col"),
    )
    out_specs = (P("row"), P(("col", "row")))
    return jax.shard_map(shards, mesh=mesh, in_specs=in_specs, out_specs=out_specs, check_vma=False)
```

profile of v0, /device:TPU:192, one launch (start us, length us, event | category | flops | bytes accessed | tf_op | source)
XLA Modules:
  0.0 226.9 jit_solution(16065609335739957065)
XLA Ops:
  0.6 0.0 copy-start
  0.6 0.8 broadcast_in_dim.147.potential_ref
  1.4 0.9 copy-done.1
  2.3 0.7 copy-done.2
  3.0 0.7 shard_map.95
  3.7 1.7 collective-permute-start
  5.4 2.9 %collective-permute-start.1 = (f32[152,128]{1,0:T(8,128)S(1)}, f32[152,128]{1,0:T(8,128)S(1)}, u32[]{:S(2)}, u32[]{:S(2)}) collective-permute-start(f32[152,128]{1,0:T(8,128)S(1)} %shard_map.95), channel_id=1, source_target_pairs={{0,32},{1,129},{2,34},{3,131},{4,36},{5,133},{6,38},{7,135},{8,40}... | collective-permute-start | bytes 233480 | tf_op jit(solution)/shard_map/ppermute | solution.py:376
  8.3 1.3 collective-permute-start.2
  9.7 1.3 fusion.19
  12.9 0.1 add_add_fusion
  13.0 0.1 sub.103
  13.8 0.0 collective-permute-done
  13.8 0.0 collective-permute-done.1
  13.8 0.0 collective-permute-done.2
  13.9 0.7 broadcast_in_dim.150
  14.6 0.1 reshape.191
  14.7 0.8 subtract_select_fusion
  15.5 0.2 compare_reduce_fusion
  15.7 0.1 convert_reduce_fusion.1
  15.8 0.7 fusion.20
  16.4 3.4 %collective-permute-start.3 = (f32[4,152,128]{2,1,0:T(8,128)S(1)}, f32[4,152,128]{2,1,0:T(8,128)S(1)}, u32[]{:S(2)}, u32[]{:S(2)}) collective-permute-start(f32[4,152,128]{2,1,0:T(8,128)S(1)} %pad_maximum_fusion.w0), channel_id=1, source_target_pairs={{1,17},{2,66},{3,19},{4,68},{6,70},{9,25},{12,76},{15,31},{17,33},... | collective-permute-start | bytes 933896 | tf_op jit(solution)/shard_map/ppermute | solution.py:376
  19.8 0.7 collective-permute-start.4
  20.5 5.2 %collective-permute-start.5 = (f32[4,152,128]{2,1,0:T(8,128)S(1)}, f32[4,152,128]{2,1,0:T(8,128)S(1)}, u32[]{:S(2)}, u32[]{:S(2)}) collective-permute-start(f32[4,152,128]{2,1,0:T(8,128)S(1)} %pad_maximum_fusion.w0), channel_id=1, source_target_pairs={{1,49},{3,51},{4,196},{5,53},{10,202},{11,59},{12,204},{14,206},{1... | collective-permute-start | bytes 933896 | tf_op jit(solution)/shard_map/ppermute | solution.py:376
  25.7 0.1 select_reduce_fusion.3
  25.8 0.1 add_select_fusion
  25.9 0.1 select_n.156
  26.0 0.3 convert_reduce_fusion
  26.3 0.6 select_reduce_fusion
  26.9 0.1 select_reduce_fusion.1
  28.3 0.1 fusion.11
  28.4 0.0 collective-permute-done.3.w1
  28.4 0.0 collective-permute-done.4.w2
  28.4 2.0 collective-permute-done.5.w3
  30.4 0.8 shard_map.97
  31.2 0.7 collective-permute-start.6
  31.9 0.0 copy-start.3
  31.9 0.8 shard_map.96
  32.7 0.0 collective-permute-done.6
  32.8 0.1 collective-permute-start.7
  32.9 0.1 fusion.1
  33.0 0.1 and.130
  33.1 0.1 and.131
  33.2 0.1 lt.150
  33.3 0.1 lt.151
  33.4 0.7 collective-permute-done.7
  34.1 0.7 collective-permute-start.8
  34.7 0.1 and_select_fusion.need_ref
  34.8 0.0 collective-permute-done.8
  34.9 0.7 collective-permute-start.11
  35.6 1.0 shard_map.98.other_ref
  36.5 0.7 collective-permute-start.10
  37.2 1.3 collective-permute-start.9
  38.5 0.1 select_reduce_fusion.2
  38.6 0.0 copy-start.4
  38.6 0.0 collective-permute-done.11.lse_ref
  38.6 0.8 shard_map.99
  39.4 0.7 all_to_all.11
  40.1 178.5 %all-to-all-start = ((f32[16,1,288]{2,1,0:T(1,128)}), f32[16,1,288]{2,1,0:T(1,128)S(1)}, u32[]{:S(2)}, u32[]{:S(2)}) async-start(f32[16,1,288]{2,1,0:T(1,128)} %all_to_all.11), calls=%async_computation | async-start | bytes 49152 | tf_op jit(solution)/shard_map/all_to_all | solution.py:499
  218.6 0.0 collective-permute-done.10
  218.6 0.0 collective-permute-done.9
  218.6 0.1 multiply_select_fusion
  218.7 0.6 reshape.192
  219.3 6.9 %all-to-all-done = f32[16,1,288]{2,1,0:T(1,128)S(1)} async-done(((f32[16,1,288]{2,1,0:T(1,128)}), f32[16,1,288]{2,1,0:T(1,128)S(1)}, u32[]{:S(2)}, u32[]{:S(2)}) %all-to-all-start) | async-done | bytes 18464 | tf_op jit(solution)/shard_map/all_to_all | solution.py:499
  226.3 0.6 add_select_fusion.2
  (28 shorter events, 0.3 us)
Async XLA Ops:
  0.6 29.8 %copy-start = (f32[4608,64]{0,1:T(8,128)S(1)}, f32[4608,64]{0,1:T(8,128)}, u32[]{:S(2)}) copy-start(f32[4608,64]{0,1:T(8,128)} %param.8) | copy-start | bytes 3538948
  1.4 0.9 copy-start.1
  2.3 0.7 copy-start.2
  3.0 23.9 %copy-start.5 = (s32[18]{0:T(128)S(1)}, s32[18]{0:T(128)}, u32[]{:S(2)}) copy-start(s32[18]{0:T(128)} %param.13) | copy-start | bytes 220
  3.7 10.1 %collective-permute-start = (f32[152,128]{1,0:T(8,128)S(1)}, f32[152,128]{1,0:T(8,128)S(1)}, u32[]{:S(2)}, u32[]{:S(2)}) collective-permute-start(f32[152,128]{1,0:T(8,128)S(1)} %shard_map.95), channel_id=1, source_target_pairs={{0,16},{1,65},{2,18},{3,67},{4,20},{5,69},{6,22},{7,71},{8,24},{9,... | collective-permute-start | bytes 233480 | tf_op jit(solution)/shard_map/ppermute | solution.py:376
  5.4 8.5 %collective-permute-start.1 = (f32[152,128]{1,0:T(8,128)S(1)}, f32[152,128]{1,0:T(8,128)S(1)}, u32[]{:S(2)}, u32[]{:S(2)}) collective-permute-start(f32[152,128]{1,0:T(8,128)S(1)} %shard_map.95), channel_id=1, source_target_pairs={{0,32},{1,129},{2,34},{3,131},{4,36},{5,133},{6,38},{7,135},{8,40}... | collective-permute-start | bytes 233480 | tf_op jit(solution)/shard_map/ppermute | solution.py:376
  8.3 5.6 %collective-permute-start.2 = (f32[152,128]{1,0:T(8,128)S(1)}, f32[152,128]{1,0:T(8,128)S(1)}, u32[]{:S(2)}, u32[]{:S(2)}) collective-permute-start(f32[152,128]{1,0:T(8,128)S(1)} %shard_map.95), channel_id=1, source_target_pairs={{0,48},{1,193},{2,50},{3,195},{4,52},{5,197},{6,54},{7,199},{8,56}... | collective-permute-start | bytes 233480 | tf_op jit(solution)/shard_map/ppermute | solution.py:376
  16.4 12.0 %collective-permute-start.3 = (f32[4,152,128]{2,1,0:T(8,128)S(1)}, f32[4,152,128]{2,1,0:T(8,128)S(1)}, u32[]{:S(2)}, u32[]{:S(2)}) collective-permute-start(f32[4,152,128]{2,1,0:T(8,128)S(1)} %pad_maximum_fusion.w0), channel_id=1, source_target_pairs={{1,17},{2,66},{3,19},{4,68},{6,70},{9,25},{12,76},{15,31},{17,33},... | collective-permute-start | bytes 933896 | tf_op jit(solution)/shard_map/ppermute | solution.py:376
  19.8 8.6 %collective-permute-start.4 = (f32[4,152,128]{2,1,0:T(8,128)S(1)}, f32[4,152,128]{2,1,0:T(8,128)S(1)}, u32[]{:S(2)}, u32[]{:S(2)}) collective-permute-start(f32[4,152,128]{2,1,0:T(8,128)S(1)} %pad_maximum_fusion.w0), channel_id=1, source_target_pairs={{0,128},{1,33},{3,35},{6,134},{8,136},{10,138},{17,49},{19,51},{21... | collective-permute-start | bytes 933896 | tf_op jit(solution)/shard_map/ppermute | solution.py:376
  20.5 9.9 %collective-permute-start.5 = (f32[4,152,128]{2,1,0:T(8,128)S(1)}, f32[4,152,128]{2,1,0:T(8,128)S(1)}, u32[]{:S(2)}, u32[]{:S(2)}) collective-permute-start(f32[4,152,128]{2,1,0:T(8,128)S(1)} %pad_maximum_fusion.w0), channel_id=1, source_target_pairs={{1,49},{3,51},{4,196},{5,53},{10,202},{11,59},{12,204},{14,206},{1... | collective-permute-start | bytes 933896 | tf_op jit(solution)/shard_map/ppermute | solution.py:376
  31.2 1.5 collective-permute-start.6
  31.9 1.3 copy-start.3
  32.8 1.3 collective-permute-start.7
  34.1 0.7 collective-permute-start.8
  34.9 3.7 %collective-permute-start.11 = (f32[18,256]{1,0:T(8,128)S(1)}, f32[18,256]{1,0:T(8,128)S(1)}, u32[]{:S(2)}, u32[]{:S(2)}) collective-permute-start(f32[18,256]{1,0:T(8,128)S(1)} %multiply_add_fusion.lse_ref), channel_id=1, source_target_pairs={{0,2},{1,8},{14,3},{15,4},{17,31},{16,25},{18,20},{19,21},{34,36},... | collective-permute-start | bytes 55304 | tf_op jit(solution)/shard_map/ppermute | solution.py:376
  36.5 182.1 %collective-permute-start.10 = (f32[18,256]{1,0:T(8,128)S(1)}, f32[18,256]{1,0:T(8,128)S(1)}, u32[]{:S(2)}, u32[]{:S(2)}) collective-permute-start(f32[18,256]{1,0:T(8,128)S(1)} %multiply_add_fusion.lse_ref), channel_id=1, source_target_pairs={{0,5},{1,6},{14,7},{15,9},{17,22},{16,23},{18,24},{19,26},{34,39},... | collective-permute-start | bytes 55304 | tf_op jit(solution)/shard_map/ppermute | solution.py:376
  37.2 181.4 %collective-permute-start.9 = (f32[18,256]{1,0:T(8,128)S(1)}, f32[18,256]{1,0:T(8,128)S(1)}, u32[]{:S(2)}, u32[]{:S(2)}) collective-permute-start(f32[18,256]{1,0:T(8,128)S(1)} %multiply_add_fusion.lse_ref), channel_id=1, source_target_pairs={{0,10},{1,11},{14,12},{15,13},{17,27},{16,28},{18,29},{19,30},{34,... | collective-permute-start | bytes 55304 | tf_op jit(solution)/shard_map/ppermute | solution.py:376
  38.6 187.7 %copy-start.4 = (f32[288]{0:T(512)S(1)}, f32[288]{0:T(512)}, u32[]{:S(2)}) copy-start(f32[288]{0:T(512)} %param.10) | copy-start | bytes 3460
  40.1 186.1 %all-to-all-start = ((f32[16,1,288]{2,1,0:T(1,128)}), f32[16,1,288]{2,1,0:T(1,128)S(1)}, u32[]{:S(2)}, u32[]{:S(2)}) async-start(f32[16,1,288]{2,1,0:T(1,128)} %all_to_all.11), calls=%async_computation | async-start | bytes 49152 | tf_op jit(solution)/shard_map/all_to_all | solution.py:499
where the time goes:
time: 228 us; the launch traced here: 227 us
  starting transfers between devices  198 us (87%)
  waiting for transfers between devices  9.58 us (4%)
  other arithmetic  5.55 us (2%)
  local copies, waits for them, and re-layouts  5.02 us (2%)
  between operations  4.96 us (2%)
  Pallas kernels  4.1 us (2%)
    all_to_all x1, starting transfers between devices, shards(): shared_out = lax.all_to_all(col_part.reshape(rows, share), 'row', 0, 0)  178 us
    ppermute x12, starting transfers between devices, send(): lax.ppermute(a, ('row', 'col'), [(s[0] * cols + s[1], d[0] * cols + d[1])...  19.2 us
    all_to_all x1, waiting for transfers between devices, shards(): shared_out = lax.all_to_all(col_part.reshape(rows, share), 'row', 0, 0)  6.9 us
  transfers between devices with their start and end apart: 13, of which 3 were waited for; matrix products, arithmetic and copies ran while one was open for 2% of the time, Pallas kernels for 1%

commit v1 on v0

--- a/solution.py
+++ b/solution.py
@@ -15,6 +15,7 @@
 floor = -1e25
 unit_rows = 64
 group = 12
+span = 8
 ring = 4
 f32 = jnp.float32
 bf16 = jnp.bfloat16
@@ -48,7 +49,7 @@
     square_ref[0:64, 0:share] = points
     turned = square_ref[...].T
     wire_ref[0:mid, :] = scale * (turned[0:mid] + pltpu.roll(turned[mid:share], 64, 1))
-    level = scale * (potential_ref[...] - 0.5 * jnp.sum(points * points, axis=0, keepdims=True))
+    level = scale * (potential_ref[...].reshape(1, share) - 0.5 * jnp.sum(points * points, axis=0, keepdims=True))
     spot = offset + lax.broadcasted_iota(jnp.int32, (1, share), 1)
     place = jnp.where(spot < tile, spot, spot - tile)
     bound = jnp.where(spot < tile, count_ref[first_tile], count_ref[last_tile])
@@ -124,51 +125,93 @@
     unpack_targets(held_ref, lambda k: copies[k].wait(), operand_ref)
 
 
-def pipeline(item_ref, list_ref, items, operand_ref, weights_ref, buffers, visit):
-    per = list_ref.shape[1] // group
-    last = weights_ref.shape[0] - 1
+def plan_work(count_ref, local_ref, plan_ref):
+    src_tiles = local_ref.shape[0] - 6
+    per_tile = 256 // unit_rows
+    units = count_ref.shape[0] * per_tile
+    per = units // group
+    unit = lax.broadcasted_iota(jnp.int32, (24, 128), 1)
+    tile_of = unit // per_tile
+    bound = jnp.zeros((24, 128), jnp.int32)
+    for t in range(count_ref.shape[0]):
+        bound = jnp.where(tile_of == t, count_ref[t], bound)
+    live = bound > (unit - tile_of * per_tile) * unit_rows
+    hits = jnp.zeros((24, 128), f32)
+    for k in range(local_ref.shape[1]):
+        hits = jnp.where(local_ref[:, k : k + 1] == tile_of, 1.0, hits)
+    active = jnp.where(live, hits, 0.0)
+    down = lax.broadcasted_iota(jnp.int32, (128, 128), 0)
+    across = lax.broadcasted_iota(jnp.int32, (128, 128), 1)
+    upto = jnp.where(down <= across, 1.0, 0.0).astype(bf16)
+    rank = jnp.dot(active.astype(bf16), upto, preferred_element_type=f32)
+    counts = jnp.broadcast_to(rank[:, 127:128], (24, 128))
+    place = jnp.where(active > 0.0, rank - 1.0, -1.0)
+    place = jnp.concatenate([place, jnp.full((104, 128), -1.0, f32)], axis=0).T
+    position = across.astype(f32)
+    value = (down - units).astype(f32)
+    plan_ref[...] = jnp.full_like(plan_ref, units)
+    last = lax.broadcasted_iota(jnp.int32, (1, 128), 1)
+    chunks = jnp.floor((counts + (group - 0.5)) / group).astype(jnp.int32)
+    begin = jnp.zeros((1, 128), jnp.int32)
+    items = jnp.full((1, 128), src_tiles * per, jnp.int32)
+    for s in range(src_tiles):
+        listed = jnp.sum(
+            jnp.where(place[:, s : s + 1] == position, value, 0.0), axis=0, keepdims=True
+        )
+        plan_ref[s : s + 1, :] = jnp.where(
+            last == 127, counts[s : s + 1], listed + units
+        ).astype(jnp.int32)
+        along = last - begin
+        inside = (along >= 0) & (along < chunks[s : s + 1])
+        items = jnp.where(inside, s * per + along, items)
+        begin = begin + chunks[s : s + 1]
+    plan_ref[src_tiles + 1 : src_tiles + 2, :] = items
+    row = lax.axis_index("row")
+    apart = lax.axis_index("col") - row + 2 - lax.rem(row, 2) + 16
+    near = jnp.where(lax.rem(apart, 16) < 4, 1, 0)
+    plan_ref[src_tiles + 2 : src_tiles + 3, :] = begin * jnp.where(last == 0, near, 1 - near)
+
+
+def pipeline(plan_ref, items, operand_ref, weights_ref, buffers, visit):
+    tiles, depth, tile = weights_ref.shape
+    per = (operand_ref.shape[0] // unit_rows - 1) // group
 
     def where(i):
-        code = item_ref[i]
+        code = plan_ref[tiles + 1, i]
         s = code // per
         first = (code - s * per) * group
-        return jnp.minimum(s, last), [list_ref[s, first + k] for k in range(group)]
-
-    def multiply(i, buffer):
-        s, units = where(i)
-        rows = jnp.concatenate(
-            [
-                operand_ref[pl.ds(pl.multiple_of(u * unit_rows, unit_rows), unit_rows), :]
-                for u in units
-            ],
-            axis=0,
-        )
-        buffer[...] = jnp.dot(rows, weights_ref[s], preferred_element_type=f32)
-
-    one, two = buffers
-    multiply(0, one)
+        return jnp.minimum(s, tiles - 1), [plan_ref[s, first + k] for k in range(group)]
 
     def step(j, carry):
-        multiply(2 * j + 1, two)
-        visit(*where(2 * j), one)
-        multiply(2 * j + 2, one)
-        visit(*where(2 * j + 1), two)
+        for k in range(span):
+            s, units = where(span * j + k)
+            rows = jnp.concatenate(
+                [
+                    operand_ref[pl.ds(pl.multiple_of(u * unit_rows, unit_rows), unit_rows), :]
+                    for u in units
+                ],
+                axis=0,
+            )
+            buffers[k][...] = jnp.dot(rows, weights_ref[s], preferred_element_type=f32)
+        for k in range(span):
+            visit(*where(span * j + k), buffers[k])
         return carry
 
-    lax.fori_loop(0, (items + 1) // 2, step, 0)
+    lax.fori_loop(0, (items + span - 1) // span, step, 0)
 
 
 def row_pass(
-    items_ref, item_ref, count_ref, list_ref, points_ref, need_ref, w0, w1, w2, w3, lse_ref,
-    held_ref, sems, operand_ref, weights_ref, one, two, total_ref,
+    which, plan_ref, points_ref, need_ref, w0, w1, w2, w3, lse_ref,
+    held_ref, sems, operand_ref, weights_ref, total_ref, *buffers,
 ):
     tiles, depth, tile = weights_ref.shape
-
-    @pl.when(items_ref[0] == 0)
+    items = plan_ref[tiles + 2, which]
+
+    @pl.when(items == 0)
     def _():
         lse_ref[...] = jnp.full_like(lse_ref, nothing)
 
-    @pl.when(items_ref[0] > 0)
+    @pl.when(items > 0)
     def _():
         load_all(points_ref, None, (w0, w1, w2, w3), held_ref, sems, operand_ref, weights_ref)
         total_ref[...] = jnp.zeros_like(total_ref)
@@ -177,7 +220,7 @@
             part = jnp.exp2(buffer[...]).reshape(4, unit_rows * group // 32, 8, tile)
             total_ref[s] += jnp.sum(jnp.sum(part, axis=1), axis=0)
 
-        pipeline(item_ref, list_ref, items_ref[0], operand_ref, weights_ref, (one, two), visit)
+        pipeline(plan_ref, items, operand_ref, weights_ref, buffers, visit)
         total = jnp.sum(total_ref[...], axis=1)
         lse_ref[...] = jnp.where(total > 0.0, jnp.log2(jnp.maximum(total, 1e-37)), nothing)
         fine = (total > 1e-25) & (total < 1e30)
@@ -190,7 +233,7 @@
 
                 def step(i, state):
                     high, total = state
-                    unit = list_ref[s, i]
+                    unit = plan_ref[s, i]
                     rows = operand_ref[
                         pl.ds(pl.multiple_of(unit * unit_rows, unit_rows), unit_rows), :
                     ]
@@ -201,7 +244,7 @@
                     return new, total + jnp.sum(jnp.exp2(score - new[None]), axis=0)
 
                 start = (jnp.full((8, tile), floor, f32), jnp.zeros((8, tile), f32))
-                high, total = lax.fori_loop(0, count_ref[s], step, start)
+                high, total = lax.fori_loop(0, plan_ref[s, 127], step, start)
                 top = jnp.max(high, axis=0, keepdims=True)
                 total = jnp.sum(total * jnp.exp2(high - top), axis=0, keepdims=True)
                 lse_ref[pl.ds(s, 1), :] = jnp.where(
@@ -213,16 +256,17 @@
 
 
 def column_pass(
-    items_ref, item_ref, count_ref, list_ref, points_ref, need_ref, w0, w1, w2, w3, lse_ref,
-    mass_ref, other_ref, out_ref, held_ref, sems, operand_ref, weights_ref, one, two, total_ref, high_ref,
+    which, plan_ref, points_ref, need_ref, w0, w1, w2, w3, lse_ref, mass_ref, other_ref, out_ref,
+    held_ref, sems, operand_ref, weights_ref, total_ref, high_ref, *buffers,
 ):
     tiles, depth, tile = weights_ref.shape
-
-    @pl.when(items_ref[0] == 0)
+    items = plan_ref[tiles + 2, which]
+
+    @pl.when(items == 0)
     def _():
         out_ref[...] = other_ref[...]
 
-    @pl.when(items_ref[0] > 0)
+    @pl.when(items > 0)
     def _():
         shift = mass_ref[...] - lse_ref[...]
         load_all(points_ref, shift, (w0, w1, w2, w3), held_ref, sems, operand_ref, weights_ref)
@@ -234,7 +278,7 @@
                 part = jnp.exp2(buffer[k * unit_rows : (k + 1) * unit_rows, :])
                 total_ref[where, :] += part[:, 0:128] + part[:, 128:256]
 
-        pipeline(item_ref, list_ref, items_ref[0], operand_ref, weights_ref, (one, two), visit)
+        pipeline(plan_ref, items, operand_ref, weights_ref, buffers, visit)
         eye = lax.broadcasted_iota(jnp.int32, (128, 128), 0) == lax.broadcasted_iota(
             jnp.int32, (128, 128), 1
         )
@@ -257,7 +301,7 @@
 
             def one_tile(s, carry):
                 def step(i, inner):
-                    unit = list_ref[s, i]
+                    unit = plan_ref[s, i]
                     where = pl.ds(pl.multiple_of(unit * unit_rows, unit_rows), unit_rows)
                     score = jnp.dot(
                         operand_ref[where, :], weights_ref[s], preferred_element_type=f32
@@ -273,7 +317,7 @@
                     )
                     return inner
 
-                lax.fori_loop(0, count_ref[s], step, 0)
+                lax.fori_loop(0, plan_ref[s, 127], step, 0)
                 return carry
 
             lax.fori_loop(0, tiles, one_tile, 0)
@@ -298,49 +342,13 @@
     return top + jnp.log2(total)
 
 
-def work_lists(partners, partner_count, dst_count, col_here):
-    src_tiles, slots = partners.shape
-    dst_tiles = dst_count.shape[0]
-    per_tile = 256 // unit_rows
-    units = dst_tiles * per_tile
-    per = -(-units // group)
-    slot_on = jnp.arange(slots, dtype=jnp.int32)[None, :] < partner_count[:, None]
-    local = jnp.where(slot_on, partners - col_here * dst_tiles, -1)
-    unit_ids = jnp.arange(units, dtype=jnp.int32)
-    unit_tile = unit_ids // per_tile
-    live = jnp.repeat(dst_count, per_tile) > (unit_ids % per_tile) * unit_rows
-    active = jnp.any(local[:, :, None] == unit_tile[None, None, :], axis=1) & live[None, :]
-    earlier = unit_ids[:, None] < unit_ids[None, :]
-    rank = jnp.sum((active[:, :, None] & earlier[None]).astype(jnp.int32), axis=1)
-    counts = jnp.sum(active.astype(jnp.int32), axis=1)
-    order = jnp.arange(per * group, dtype=jnp.int32)
-    listed = jnp.sum(
-        jnp.where(
-            active[:, :, None] & (rank[:, :, None] == order[None, None, :]),
-            unit_ids[None, :, None] - units,
-            0,
-        ),
-        axis=1,
-    ) + units
-    listed = jnp.concatenate([listed, jnp.full((1, per * group), units, jnp.int32)], axis=0)
-    chunks = (counts + group - 1) // group
-    tile_ids = jnp.arange(src_tiles, dtype=jnp.int32)
-    first = jnp.sum(jnp.where(tile_ids[None, :] < tile_ids[:, None], chunks[None, :], 0), axis=1)
-    within = jnp.arange(per, dtype=jnp.int32)
-    spot = jnp.where(within[None, :] < chunks[:, None], first[:, None] + within[None, :], -1)
-    code = tile_ids[:, None] * per + within[None, :] - src_tiles * per
-    length = src_tiles * per + 2
-    hit = spot.reshape(-1)[:, None] == jnp.arange(length, dtype=jnp.int32)[None, :]
-    items = jnp.sum(jnp.where(hit, code.reshape(-1)[:, None], 0), axis=0) + src_tiles * per
-    wanted = jnp.any(local[:, :, None] == jnp.arange(dst_tiles, dtype=jnp.int32), axis=1)
-    return jnp.sum(chunks), items, counts, listed, wanted
-
-
 def roles(parity, cols):
     four = [d % cols for d in ((-2, -1, 0, 1), (-1, 0, 1, 2))[parity]]
     lead = [0, (1, -1)[parity] % cols]
     near = lead + [d for d in four if d not in lead]
     out = [(2, -2)[parity] % cols, cols // 2]
+    begin = four[0]
+    out += [(begin + 5) % cols, (begin + 6) % cols]
     return near, out + [d for d in range(cols) if d not in near and d not in out]
 
 
@@ -348,6 +356,7 @@
     src_tiles = src_count.shape[0]
     dst_tiles = dst_count.shape[0]
     tile = src_points.shape[0] // src_tiles
+    slots = partners.shape[1]
     rows = lax.axis_size("row")
     cols = lax.axis_size("col")
     row_here = lax.axis_index("row")
@@ -361,16 +370,15 @@
     places = [roles(r % 2, cols) for r in range(rows)]
     near = [[(r + d) % cols for d in places[r][0]] for r in range(rows)]
     far = [[(r + d) % cols for d in places[r][1]] for r in range(rows)]
-    turn = [
-        0 if d in places[p][0] else 1 + places[p][1].index(d) // 4
-        for p in range(2)
-        for d in range(cols)
-    ]
-    at = row_here % 2 * cols + (col_here - row_here) % cols
-    role = jnp.sum(
-        jnp.where(jnp.arange(2 * cols) == at, jnp.array(turn, jnp.int32), 0), dtype=jnp.int32
-    )
-    in_near = role == 0
+    parity = lax.rem(row_here, 2)
+    apart = lax.rem(col_here - row_here + 2 - parity + cols, cols)
+    in_near = apart < 4
+    in_far = (
+        (apart == 5)
+        | (apart == 6)
+        | (apart == jnp.where(parity == 0, 4, cols - 1))
+        | (apart == jnp.where(parity == 0, 10, 9))
+    )
 
     def send(a, hops):
         return lax.ppermute(a, ("row", "col"), [(s[0] * cols + s[1], d[0] * cols + d[1]) for s, d in hops])
@@ -384,7 +392,7 @@
         out_specs=vmem,
         scratch_shapes=[pltpu.VMEM((128, 384), f32), pltpu.VMEM((8, 384), f32)],
         compiler_params=params,
-    )(dst_count, dst_points.T, dst_potential[None, :])
+    )(dst_count, dst_points.T, dst_potential)
 
     def around(r, dx, dy):
         return (r // ring + dx) % ring * ring + (r + dy) % ring
@@ -399,10 +407,19 @@
         [wire]
         + [send(wire, [((r, c), (first_hop(r, c, k), c)) for r, c in every]) for k in (1, 2, 3)]
     )
-    bundle, partners, partner_count, dst_count, src_count = lax.optimization_barrier(
-        (bundle, partners, partner_count, dst_count, src_count)
-    )
     busy = [set(near[r] + far[r][:2]) for r in range(rows)]
+    slot_on = jnp.arange(slots, dtype=jnp.int32)[None, :] < partner_count[:, None]
+    local = jnp.where(slot_on, partners - col_here * dst_tiles, -1)
+    plan = pl.pallas_call(
+        plan_work,
+        out_shape=jax.ShapeDtypeStruct((24, 128), jnp.int32),
+        in_specs=[smem, vmem],
+        out_specs=vmem,
+        compiler_params=params,
+    )(dst_count, jnp.pad(local, ((0, 24 - src_tiles), (0, 0)), constant_values=-1))
+    plan, local, dst_count, src_count, bundle = lax.optimization_barrier(
+        (plan, local, dst_count, src_count, bundle)
+    )
     wires = [bundle] + [
         send(
             bundle,
@@ -414,16 +431,11 @@
         )
         for k in (1, 2, 3)
     ]
-
-    total_items, items, counts, listed, wanted = work_lists(
-        partners, partner_count, dst_count, col_here
-    )
-    near_items = jnp.where(in_near, total_items, 0)[None]
-    far_items = jnp.where(in_near, 0, total_items)[None]
     place = jnp.arange(tile, dtype=jnp.int32)
     src_live = place[None, :] < src_count[:, None]
     dst_live = place[None, :] < dst_count[:, None]
-    src_need = jnp.where(src_live & (counts > 0)[:, None], 1.0, 0.0)
+    wanted = jnp.any(local[:, :, None] == jnp.arange(dst_tiles, dtype=jnp.int32), axis=1)
+    src_need = jnp.where(src_live & jnp.any(wanted, axis=1)[:, None], 1.0, 0.0)
     dst_need = jnp.where(dst_live & jnp.any(wanted, axis=0)[:, None], 1.0, 0.0)
     dst_need = dst_need.reshape(points // 128, 128)
     counted = src_count.astype(f32)
@@ -435,72 +447,64 @@
         pltpu.SemaphoreType.DMA((ring,)),
         pltpu.VMEM((points + unit_rows, 256), bf16),
         pltpu.VMEM((src_tiles, 256, tile), bf16),
-        pltpu.VMEM((unit_rows * group, tile), f32),
-        pltpu.VMEM((unit_rows * group, tile), f32),
     ]
+    buffers = [pltpu.VMEM((unit_rows * group, tile), f32)] * span
     heavy = pl.CostEstimate(flops=8_000_000_000, bytes_accessed=4_000_000, transcendentals=8_000_000)
     light = pl.CostEstimate(flops=100_000_000, bytes_accessed=100_000, transcendentals=100_000)
     turned = src_points.T
 
-    def sum_rows(amount, cost):
+    def sum_rows(which, cost):
         return pl.pallas_call(
-            row_pass,
+            functools.partial(row_pass, which),
             out_shape=jax.ShapeDtypeStruct((src_tiles, tile), f32),
-            in_specs=[smem] * 4 + [vmem] * 2 + [anywhere] * ring,
+            in_specs=[smem] + [vmem] * 2 + [anywhere] * ring,
             out_specs=vmem,
-            scratch_shapes=scratch + [pltpu.VMEM((src_tiles, 8, tile), f32)],
+            scratch_shapes=scratch + [pltpu.VMEM((src_tiles, 8, tile), f32)] + buffers,
             compiler_params=params,
             cost_estimate=cost,
-        )(amount, items, counts, listed, turned, src_need, *wires)
-
-    def sum_columns(amount, lse, other, cost):
+        )(plan, turned, src_need, *wires)
+
+    def sum_columns(which, lse, other, cost):
         return pl.pallas_call(
-            column_pass,
+            functools.partial(column_pass, which),
             out_shape=jax.ShapeDtypeStruct((points // 128, 128), f32),
-            in_specs=[smem] * 4 + [vmem] * 2 + [anywhere] * ring + [vmem] * 3,
+            in_specs=[smem] + [vmem] * 2 + [anywhere] * ring + [vmem] * 3,
             out_specs=vmem,
-            scratch_shapes=scratch + [pltpu.VMEM((points + unit_rows, 128), f32)] * 2,
+            scratch_shapes=scratch + [pltpu.VMEM((points + unit_rows, 128), f32)] * 2 + buffers,
             compiler_params=params,
             cost_estimate=cost,
-        )(amount, items, counts, listed, turned, dst_need, *wires, lse, mass, other)
-
-    far_lse = sum_rows(far_items, light)
+        )(plan, turned, dst_need, *wires, lse, mass, other)
+
+    far_lse = sum_rows(1, light)
     early = send(far_lse, [((r, far[r][k]), (r, near[r][k])) for r in range(rows) for k in (0, 1)])
-    near_lse = sum_rows(near_items, heavy)
-    got_early = (col_here == row_here) | (col_here == row_here + 1 - 2 * (row_here % 2))
+    near_lse = sum_rows(0, heavy)
+    got_early = (col_here == row_here) | (col_here == row_here + 1 - 2 * parity)
     lse = log_sum([near_lse, jnp.where(got_early, early, nothing)])
-    lse = log_sum([lse, send(lse, [((r, c), (r, c ^ 1)) for r, c in every])])
+
+    def pairs(test):
+        return [((r, c), (r, d)) for r in range(rows) for c in near[r] for d in near[r] if test(c, d)]
+
     lse = log_sum(
         [
             lse,
-            send(
-                lse,
-                [
-                    ((r, c), (r, d))
-                    for r in range(rows)
-                    for c in near[r]
-                    for d in near[r]
-                    if (c - d) % cols in (2, cols - 2)
-                ],
-            ),
+            send(lse, [((r, c), (r, c ^ 1)) for r, c in every]),
+            send(lse, pairs(lambda c, d: (c - d) % cols in (2, cols - 2))),
+            send(lse, pairs(lambda c, d: (c - (d ^ 1)) % cols in (2, cols - 2))),
         ]
     )
-    def final(a, j):
-        return send(
-            a, [((r, near[r][k]), (r, far[r][4 * j + k])) for r in range(rows) for k in range(4)]
-        )
-
+    spread = send(lse, [((r, near[r][k]), (r, far[r][k])) for r in range(rows) for k in range(4)])
     blank = jnp.full((points // 128, 128), nothing, f32)
-    finals = [final(lse, 0)]
-    near_part = sum_columns(near_items, lse, blank, heavy)
-    late, near_part = lax.optimization_barrier((lse, near_part))
-    finals += [final(late, 1), final(late, 2)]
-    col_part = sum_columns(far_items, finals[0], near_part, light)
+    near_part = sum_columns(0, lse, blank, heavy)
+    col_part = sum_columns(1, spread, near_part, light)
+    known = jnp.where(in_far, spread, lse)
+    known, near_part = lax.optimization_barrier((known, near_part))
+    rest = send(
+        known,
+        [((r, (near[r] + far[r])[k]), (r, far[r][4 + k])) for r in range(rows) for k in range(8)],
+    )
     shared_out = lax.all_to_all(col_part.reshape(rows, share), "row", 0, 0)
 
-    row_lse = lse
-    for j in range(3):
-        row_lse = jnp.where(role == j + 1, finals[j], row_lse)
+    row_lse = jnp.where(in_near | in_far, known, rest)
     src_potential = jnp.where(
         src_live,
         entropy * (-jnp.log(counted)[:, None] - math.log(all_src) - ln2 * row_lse),

time: 228 us -> 232 us (1.018)
  the two profiles are of different devices: /device:TPU:192 before, /device:TPU:116 now
where the time goes in v1:
time: 232 us; the launch traced here: 227 us
  starting transfers between devices  202 us (87%)
  waiting for transfers between devices  9.8 us (4%)
  Pallas kernels  5.45 us (2%)
  local copies, waits for them, and re-layouts  5.34 us (2%)
  other arithmetic  3.66 us (2%)
    all_to_all x1, starting transfers between devices, shards(): shared_out = lax.all_to_all(col_part.reshape(rows, share), 'row', 0, 0)  187 us
    ppermute x12, starting transfers between devices, send(): lax.ppermute(a, ('row', 'col'), [(s[0] * cols + s[1], d[0] * cols + d[1])...  14.9 us
    ppermute x12, waiting for transfers between devices, send(): lax.ppermute(a, ('row', 'col'), [(s[0] * cols + s[1], d[0] * cols + d[1])...  7.46 us
  transfers between devices with their start and end apart: 13, of which 5 were waited for; matrix products, arithmetic and copies ran while one was open for 2% of the time, Pallas kernels for 1%

profile of v1, /device:TPU:116, one launch (start us, length us, event | category | flops | bytes accessed | tf_op | source)
XLA Modules:
  0.0 227.5 jit_solution(12465603888750408888)
XLA Ops:
  0.6 0.0 copy-start
  0.6 0.0 copy-start.1
  0.6 1.0 copy-done.1
  1.6 0.0 copy-start.2
  1.6 0.7 copy-done.2
  2.3 0.0 copy-start.4
  2.3 0.7 copy-done.4
  3.0 0.7 shard_map.87
  3.7 1.4 collective-permute-start
  5.1 0.6 collective-permute-start.1
  5.7 1.1 collective-permute-start.2
  6.7 0.8 subtract_select_fusion
  7.5 0.0 copy-start.5
  7.5 0.6 copy-done.5
  8.2 1.4 shard_map.86.plan_ref
  9.7 0.0 collective-permute-done
  9.7 1.3 collective-permute-done.1
  11.0 0.1 collective-permute-done.2
  11.1 3.1 %collective-permute-start.3 = (f32[4,152,128]{2,1,0:T(8,128)S(1)}, f32[4,152,128]{2,1,0:T(8,128)S(1)}, u32[]{:S(2)}, u32[]{:S(2)}) collective-permute-start(f32[4,152,128]{2,1,0:T(8,128)S(1)} %pad_maximum_fusion.w0), channel_id=1, source_target_pairs={{1,17},{2,66},{3,19},{4,68},{6,70},{9,25},{12,76},{15,31},{17,33},... | collective-permute-start | bytes 933896 | tf_op jit(solution)/shard_map/ppermute | solution.py:384
  14.2 0.7 collective-permute-start.4
  14.9 4.0 %collective-permute-start.5 = (f32[4,152,128]{2,1,0:T(8,128)S(1)}, f32[4,152,128]{2,1,0:T(8,128)S(1)}, u32[]{:S(2)}, u32[]{:S(2)}) collective-permute-start(f32[4,152,128]{2,1,0:T(8,128)S(1)} %pad_maximum_fusion.w0), channel_id=1, source_target_pairs={{1,49},{3,51},{4,196},{5,53},{10,202},{11,59},{12,204},{14,206},{1... | collective-permute-start | bytes 933896 | tf_op jit(solution)/shard_map/ppermute | solution.py:384
  18.9 0.5 fusion
  19.4 0.7 lt.70
  20.1 0.1 lt.71
  20.2 0.1 and.43
  20.2 0.1 and.44
  20.4 0.1 and_select_fusion.need_ref
  20.4 0.7 negate_add_fusion.1
  21.1 0.7 fusion.7
  21.8 0.0 collective-permute-done.3.w1
  21.9 0.0 collective-permute-done.4.w2
  21.9 2.2 collective-permute-done.5.w3
  24.1 0.0 copy-done
  24.1 0.8 shard_map.89
  24.9 0.0 copy-start.6
  24.9 0.7 collective-permute-start.6
  25.6 0.8 shard_map.88
  26.3 0.0 collective-permute-done.6
  26.4 0.1 collective-permute-start.7
  26.5 0.7 collective-permute-start.8
  27.2 0.7 collective-permute-start.9
  27.8 0.0 copy-done.6
  27.9 0.1 select_reduce_fusion
  27.9 0.0 collective-permute-done.7
  27.9 0.0 collective-permute-done.8
  28.0 0.0 collective-permute-done.9
  28.0 0.7 collective-permute-start.10
  28.7 1.0 shard_map.90.other_ref
  29.7 0.0 copy-start.3
  29.7 0.0 copy-start.7
  29.7 0.0 collective-permute-done.10.lse_ref
  29.7 0.8 shard_map.91
  30.5 0.7 all_to_all.11
  31.2 187.4 %all-to-all-start = ((f32[16,1,288]{2,1,0:T(1,128)}), f32[16,1,288]{2,1,0:T(1,128)S(1)}, u32[]{:S(2)}, u32[]{:S(2)}) async-start(f32[16,1,288]{2,1,0:T(1,128)} %all_to_all.11), calls=%async_computation | async-start | bytes 49152 | tf_op jit(solution)/shard_map/all_to_all | solution.py:505
  218.6 1.3 collective-permute-start.11
  219.9 2.3 %all-to-all-done = f32[16,1,288]{2,1,0:T(1,128)S(1)} async-done(((f32[16,1,288]{2,1,0:T(1,128)}), f32[16,1,288]{2,1,0:T(1,128)S(1)}, u32[]{:S(2)}, u32[]{:S(2)}) %all-to-all-start) | async-done | bytes 18464 | tf_op jit(solution)/shard_map/all_to_all | solution.py:505
  222.3 0.0 copy-done.3
  222.3 0.6 add_select_fusion.1
  222.9 3.8 %collective-permute-done.11 = f32[18,256]{1,0:T(8,128)S(1)} collective-permute-done((f32[18,256]{1,0:T(8,128)S(1)}, f32[18,256]{1,0:T(8,128)S(1)}, u32[]{:S(2)}, u32[]{:S(2)}) %collective-permute-start.11) | collective-permute-done | bytes 18464 | tf_op jit(solution)/shard_map/ppermute | solution.py:384
  226.8 0.0 copy-done.7
  226.8 0.1 multiply_select_fusion
  226.9 0.6 reshape.49
  (12 shorter events, 0.2 us)
Async XLA Ops:
  0.6 23.5 %copy-start = (f32[4608,64]{0,1:T(8,128)S(1)}, f32[4608,64]{0,1:T(8,128)}, u32[]{:S(2)}) copy-start(f32[4608,64]{0,1:T(8,128)} %param.7) | copy-start | bytes 3538948
  0.6 1.0 copy-start.1
  1.6 0.7 copy-start.2
  2.3 0.7 copy-start.4
  3.7 6.0 %collective-permute-start = (f32[152,128]{1,0:T(8,128)S(1)}, f32[152,128]{1,0:T(8,128)S(1)}, u32[]{:S(2)}, u32[]{:S(2)}) collective-permute-start(f32[152,128]{1,0:T(8,128)S(1)} %shard_map.87), channel_id=1, source_target_pairs={{0,16},{1,65},{2,18},{3,67},{4,20},{5,69},{6,22},{7,71},{8,24},{9,... | collective-permute-start | bytes 233480 | tf_op jit(solution)/shard_map/ppermute | solution.py:384
  5.1 5.9 %collective-permute-start.1 = (f32[152,128]{1,0:T(8,128)S(1)}, f32[152,128]{1,0:T(8,128)S(1)}, u32[]{:S(2)}, u32[]{:S(2)}) collective-permute-start(f32[152,128]{1,0:T(8,128)S(1)} %shard_map.87), channel_id=1, source_target_pairs={{0,32},{1,129},{2,34},{3,131},{4,36},{5,133},{6,38},{7,135},{8,40}... | collective-permute-start | bytes 233480 | tf_op jit(solution)/shard_map/ppermute | solution.py:384
  5.7 5.4 %collective-permute-start.2 = (f32[152,128]{1,0:T(8,128)S(1)}, f32[152,128]{1,0:T(8,128)S(1)}, u32[]{:S(2)}, u32[]{:S(2)}) collective-permute-start(f32[152,128]{1,0:T(8,128)S(1)} %shard_map.87), channel_id=1, source_target_pairs={{0,48},{1,193},{2,50},{3,195},{4,52},{5,197},{6,54},{7,199},{8,56}... | collective-permute-start | bytes 233480 | tf_op jit(solution)/shard_map/ppermute | solution.py:384
  7.5 0.7 copy-start.5
  11.1 10.8 %collective-permute-start.3 = (f32[4,152,128]{2,1,0:T(8,128)S(1)}, f32[4,152,128]{2,1,0:T(8,128)S(1)}, u32[]{:S(2)}, u32[]{:S(2)}) collective-permute-start(f32[4,152,128]{2,1,0:T(8,128)S(1)} %pad_maximum_fusion.w0), channel_id=1, source_target_pairs={{1,17},{2,66},{3,19},{4,68},{6,70},{9,25},{12,76},{15,31},{17,33},... | collective-permute-start | bytes 933896 | tf_op jit(solution)/shard_map/ppermute | solution.py:384
  14.2 7.6 %collective-permute-start.4 = (f32[4,152,128]{2,1,0:T(8,128)S(1)}, f32[4,152,128]{2,1,0:T(8,128)S(1)}, u32[]{:S(2)}, u32[]{:S(2)}) collective-permute-start(f32[4,152,128]{2,1,0:T(8,128)S(1)} %pad_maximum_fusion.w0), channel_id=1, source_target_pairs={{0,128},{1,33},{3,35},{6,134},{8,136},{10,138},{17,49},{19,51},{21... | collective-permute-start | bytes 933896 | tf_op jit(solution)/shard_map/ppermute | solution.py:384
  14.9 9.2 %collective-permute-start.5 = (f32[4,152,128]{2,1,0:T(8,128)S(1)}, f32[4,152,128]{2,1,0:T(8,128)S(1)}, u32[]{:S(2)}, u32[]{:S(2)}) collective-permute-start(f32[4,152,128]{2,1,0:T(8,128)S(1)} %pad_maximum_fusion.w0), channel_id=1, source_target_pairs={{1,49},{3,51},{4,196},{5,53},{10,202},{11,59},{12,204},{14,206},{1... | collective-permute-start | bytes 933896 | tf_op jit(solution)/shard_map/ppermute | solution.py:384
  24.9 3.0 %copy-start.6 = (s32[18]{0:T(128)S(1)}, s32[18]{0:T(128)}, u32[]{:S(2)}) copy-start(s32[18]{0:T(128)} %count_ref.3) | copy-start | bytes 220
  24.9 1.5 collective-permute-start.6
  26.4 1.5 collective-permute-start.7
  26.5 1.5 collective-permute-start.8
  27.2 0.8 collective-permute-start.9
  28.0 1.7 collective-permute-start.10
  29.7 192.6 %copy-start.3 = (f32[288]{0:T(512)S(1)}, f32[288]{0:T(512)}, u32[]{:S(2)}) copy-start(f32[288]{0:T(512)} %potential_ref.1) | copy-start | bytes 3460
  29.7 197.1 %copy-start.7 = (s32[18]{0:T(128)S(1)}, s32[18]{0:T(128)}, u32[]{:S(2)}) copy-start(s32[18]{0:T(128)} %param.12) | copy-start | bytes 220
  31.2 191.0 %all-to-all-start = ((f32[16,1,288]{2,1,0:T(1,128)}), f32[16,1,288]{2,1,0:T(1,128)S(1)}, u32[]{:S(2)}, u32[]{:S(2)}) async-start(f32[16,1,288]{2,1,0:T(1,128)} %all_to_all.11), calls=%async_computation | async-start | bytes 49152 | tf_op jit(solution)/shard_map/all_to_all | solution.py:505
  218.6 8.2 %collective-permute-start.11 = (f32[18,256]{1,0:T(8,128)S(1)}, f32[18,256]{1,0:T(8,128)S(1)}, u32[]{:S(2)}, u32[]{:S(2)}) collective-permute-start(f32[18,256]{1,0:T(8,128)S(1)} %broadcast_select_fusion), channel_id=1, source_target_pairs={{0,5},{1,6},{14,7},{15,9},{2,10},{8,11},{3,12},{4,13},{17,20},{16,... | collective-permute-start | bytes 55304 | tf_op jit(solution)/shard_map/ppermute | solution.py:384
